TPU v7x, 32 devices: a whole 2x2x4 slice. The times are simulated.
32 devices in a mesh: tile: 8 (over z, x), filt: 4 (over y, core).
Axes of the slice: x: 2, y: 2, z: 4, core: 2. Of those that a mesh axis runs over, the one named last changes fastest.
Arguments:
- panels: bfloat16 [64, 12, 512], P('tile', None, 'filt'), may hold values from -12 to 12
- panel_tile: int32 [64, 1], P('tile'), may hold values from 0 to 7; in each aligned block of 8 rows (0 to 7, 8 to 15, ...) at most 2 rows name the same one
- panel_date: int32 [64], P('tile'), may hold values from 0 to 1
- stem_weight: bfloat16 [12, 128], replicated, may hold values from -1.75 to 1.75
- spatial_weight: bfloat16 [3, 3, 128, 128], P(None, None, None, 'filt'), may hold values from -0.1875 to 0.1875
- temporal_weight: bfloat16 [3, 128, 128], P(None, None, 'filt'), may hold values from -0.3125 to 0.3125
- cotangent: bfloat16 [2, 128, 32, 128], P(None, 'filt', 'tile'), may hold values from -6 to 6
Outputs:
- features_out: bfloat16 [2, 128, 32, 128], P(None, 'filt', 'tile')
- grad_stem: float32 [12, 128], replicated
- grad_spatial: float32 [3, 3, 128, 128], P(None, None, None, 'filt')
- grad_temporal: float32 [3, 128, 128], P(None, None, 'filt')
- band_grad: float32 [2, 12, 4096], P(None, None, ('tile', 'filt'))
Inputs may be any that keep to these rules, and one draw needn't show every extreme that they name: `panel_tile`: among the panels of one reader (aligned blocks of 8 rows) no tile is named more than 2 times, a bound that some block reaches.
All inputs are finite; a program needn't handle non-finite values.
Results may differ from a plain program's by a relative error of at most 0.015.
Values may be sent and summed in bfloat16 or wider, within the bound.
A program may use at most 64 MiB of HBM per device.

v0:
```python
import math

import jax
import jax.numpy as jnp
from jax import lax
from jax.sharding import PartitionSpec as P

CAP = 2


def padded(cells, sides, width):
    for axis, dim in sides:
        count = lax.axis_size(axis)
        ends = count - 1
        head = lax.slice_in_dim(cells, 0, width, axis=dim)
        tail = lax.slice_in_dim(cells, cells.shape[dim] - width, cells.shape[dim], axis=dim)
        cells = jnp.concatenate(
            [
                lax.ppermute(tail, axis, [(i, (i + 1) % count) for i in range(ends)]),
                cells,
                lax.ppermute(head, axis, [((i + 1) % count, i) for i in range(ends)]),
            ],
            axis=dim,
        )
    return cells


def shift_cols(values, offset):
    if offset == 0:
        return values
    zero_col = jnp.zeros(values.shape[:-1] + (1,), values.dtype)
    if offset == 1:
        return jnp.concatenate([values[..., 1:], zero_col], axis=-1)
    return jnp.concatenate([zero_col, values[..., :-1]], axis=-1)


def silu_slope(pre_act):
    sigma = jax.nn.sigmoid(pre_act)
    return sigma * (1.0 + pre_act * (1.0 - sigma))


def per_device(
    panels, panel_tile, panel_date, stem_weight, spatial_weight, temporal_weight, cotangent
):
    n_tile = lax.axis_size("tile")
    filt_id = lax.axis_index("filt")
    n_slots, n_bands, quarter = panels.shape
    n_dates, own_chan, n_rows, n_cols = cotangent.shape
    n_chan = stem_weight.shape[1]
    own_start = filt_id * own_chan
    highest = lax.Precision.HIGHEST
    stem_float = stem_weight.astype(jnp.float32)
    dest_tile = panel_tile[:, 0]
    onehot = (dest_tile[:, None] == jnp.arange(n_tile, dtype=jnp.int32)[None, :]).astype(jnp.int32)
    before = jnp.cumsum(onehot, axis=0) - onehot
    slot_rank = jnp.sum(before * onehot, axis=1)
    slot_id = dest_tile * CAP + slot_rank
    selector = slot_id[None, :] == jnp.arange(n_tile * CAP, dtype=jnp.int32)[:, None]
    outgoing = jnp.dot(
        selector.astype(jnp.bfloat16),
        panels.reshape(n_slots, n_bands * quarter),
        preferred_element_type=jnp.float32,
    ).astype(jnp.bfloat16)
    out_dates = jnp.sum(jnp.where(selector, panel_date[None, :] + 1, 0), axis=1) - 1
    arrived, arrived_dates = (
        lax.all_to_all(
            outgoing.reshape(n_tile, CAP * n_bands * quarter),
            "tile",
            split_axis=0,
            concat_axis=0,
            tiled=True,
        ),
        lax.all_to_all(
            out_dates.reshape(n_tile, CAP), "tile", split_axis=0, concat_axis=0, tiled=True
        ),
    )
    picker = arrived_dates.reshape(-1)[None, :] == jnp.arange(n_dates, dtype=jnp.int32)[:, None]
    totals = jnp.dot(
        picker.astype(jnp.bfloat16),
        arrived.reshape(n_tile * CAP, n_bands * quarter),
        preferred_element_type=jnp.float32,
    )
    counts = jnp.sum(picker.astype(jnp.float32), axis=1)
    raw_bands = (
        (totals / jnp.maximum(counts, 1.0)[:, None])
        .astype(jnp.bfloat16)
        .reshape(n_dates, n_bands, quarter)
    )
    feat_quarter = jnp.einsum(
        "bc,tbp->tcp", stem_weight, raw_bands, preferred_element_type=jnp.float32
    ).astype(jnp.bfloat16)
    feat_tile = lax.all_gather(feat_quarter, "filt", axis=2, tiled=True).reshape(
        n_dates, n_chan, n_rows, n_cols
    )
    feat_halo = padded(feat_tile, (("tile", 2),), 1)
    own_feats = lax.dynamic_slice_in_dim(feat_tile, own_start, own_chan, 1)
    shifted = [shift_cols(feat_halo, col_off - 1) for col_off in range(3)]
    pre_act = jnp.zeros((n_dates, own_chan, n_rows, n_cols), jnp.float32)
    for row_off in range(3):
        for col_off in range(3):
            pre_act = pre_act + jnp.einsum(
                "tirw,io->torw",
                shifted[col_off][:, :, row_off : row_off + n_rows],
                spatial_weight[row_off, col_off],
                preferred_element_type=jnp.float32,
            )
    activated = jax.nn.silu(pre_act).astype(jnp.bfloat16)
    act_full = lax.all_gather(activated, "filt", axis=1, tiled=True)
    zero_date = jnp.zeros((1, n_chan, n_rows, n_cols), jnp.bfloat16)
    act_pad = jnp.concatenate([zero_date, act_full, zero_date], axis=0)
    temporal_out = jnp.zeros((n_dates, own_chan, n_rows, n_cols), jnp.float32)
    for lag in range(3):
        temporal_out = temporal_out + jnp.einsum(
            "tirw,io->torw",
            act_pad[lag : lag + n_dates],
            temporal_weight[lag],
            preferred_element_type=jnp.float32,
        )
    features_out = (own_feats.astype(jnp.float32) + temporal_out).astype(jnp.bfloat16)
    grad_scale = 1.0 / math.sqrt(n_dates * n_rows * n_tile * n_cols)
    temporal_terms = jnp.stack(
        [
            jnp.einsum(
                "tirw,torw->io",
                act_pad[lag : lag + n_dates],
                cotangent,
                preferred_element_type=jnp.float32,
            )
            for lag in range(3)
        ]
    )
    zero_grad = jnp.zeros((1, own_chan, n_rows, n_cols), jnp.bfloat16)
    grad_pad = jnp.concatenate([zero_grad, cotangent, zero_grad], axis=0)
    back_part = jnp.zeros((n_dates, n_chan, n_rows, n_cols), jnp.float32)
    for lag in range(3):
        back_part = back_part + jnp.einsum(
            "torw,io->tirw",
            grad_pad[2 - lag : 2 - lag + n_dates],
            temporal_weight[lag],
            preferred_element_type=jnp.float32,
        )
    act_grad = lax.psum_scatter(
        back_part.astype(jnp.bfloat16), "filt", scatter_dimension=1, tiled=True
    ).astype(jnp.float32)
    pre_grad = (act_grad * silu_slope(pre_act)).astype(jnp.bfloat16)
    spatial_terms = jnp.stack(
        [
            jnp.stack(
                [
                    jnp.einsum(
                        "tirw,torw->io",
                        shifted[col_off][:, :, row_off : row_off + n_rows],
                        pre_grad,
                        preferred_element_type=jnp.float32,
                    )
                    for col_off in range(3)
                ]
            )
            for row_off in range(3)
        ]
    )
    pre_halo = padded(pre_grad, (("tile", 2),), 1)
    pre_shift = [shift_cols(pre_halo, 1 - col_off) for col_off in range(3)]
    feat_part = jnp.zeros((n_dates, n_chan, n_rows, n_cols), jnp.float32)
    for row_off in range(3):
        for col_off in range(3):
            feat_part = feat_part + jnp.einsum(
                "torw,io->tirw",
                pre_shift[col_off][:, :, 2 - row_off : 2 - row_off + n_rows],
                spatial_weight[row_off, col_off],
                preferred_element_type=jnp.float32,
            )
    own_part = lax.dynamic_slice_in_dim(feat_part, own_start, own_chan, 1) + cotangent.astype(
        jnp.float32
    )
    feat_part = lax.dynamic_update_slice_in_dim(feat_part, own_part, own_start, 1)
    feat_grad = lax.psum_scatter(
        feat_part.reshape(n_dates, n_chan, n_rows * n_cols).astype(jnp.bfloat16),
        "filt",
        scatter_dimension=2,
        tiled=True,
    ).astype(jnp.float32)
    grad_upper = feat_grad.astype(jnp.bfloat16)
    grad_lower = (feat_grad - grad_upper.astype(jnp.float32)).astype(jnp.bfloat16)
    stem_part = jnp.einsum(
        "tbp,tcp->bc", raw_bands, grad_upper, preferred_element_type=jnp.float32
    ) + jnp.einsum("tbp,tcp->bc", raw_bands, grad_lower, preferred_element_type=jnp.float32)
    band_grad = jnp.einsum("bc,tcp->tbp", stem_float, feat_grad, precision=highest)
    grad_stem = lax.psum(stem_part * grad_scale, ("tile", "filt"))
    grad_spatial, grad_temporal = lax.psum(
        (spatial_terms * grad_scale, temporal_terms * grad_scale), "tile"
    )
    return (features_out, grad_stem, grad_spatial, grad_temporal, band_grad)


def solution(mesh):
    in_specs = (
        P("tile", None, "filt"),
        P("tile", None),
        P("tile"),
        P(),
        P(None, None, None, "filt"),
        P(None, None, "filt"),
        P(None, "filt", "tile", None),
    )
    out_specs = (
        P(None, "filt", "tile", None),
        P(),
        P(None, None, None, "filt"),
        P(None, None, "filt"),
        P(None, None, ("tile", "filt")),
    )
    return jax.shard_map(
        per_device, mesh=mesh, in_specs=in_specs, out_specs=out_specs, check_vma=False
    )
```

profile of v0, /device:TPU:0, one launch (start us, length us, event | category | flops | bytes accessed | tf_op | source)
XLA Modules:
  0.0 187.9 jit_solution(6536387196281619419)
XLA Ops:
  8.9 0.7 sub.16
  9.6 7.3 %all-to-all-start = ((s32[8,1,2]{2,1,0:T(1,128)}), s32[8,1,2]{2,1,0:T(1,128)S(1)}, u32[]{:S(2)}, u32[]{:S(2)}) async-start(s32[8,1,2]{2,1,0:T(1,128)} %bitcast.1), calls=%async_computation | async-start | bytes 8192 | tf_op jit(solution)/shard_map/all_to_all | solution.py:73
  16.9 1.0 convolution_bitcast_fusion.1
  18.2 1.0 fusion.5
  20.0 0.9 reduce.5
  21.5 1.7 all-to-all-done
  23.2 4.3 %all-to-all-start.1 = ((bf16[8,2,1536]{2,1,0:T(2,128)(2,1)}), bf16[8,2,1536]{2,1,0:T(2,128)(2,1)S(1)}, u32[]{:S(2)}, u32[]{:S(2)}) async-start(bf16[8,2,1536]{2,1,0:T(2,128)(2,1)} %reshape.103), calls=%async_computation.1 | async-start | bytes 98304 | tf_op jit(solution)/shard_map/all_to_all | solution.py:66
  29.0 5.4 %all-to-all-done.1 = bf16[8,2,1536]{2,1,0:T(2,128)(2,1)S(1)} async-done(((bf16[8,2,1536]{2,1,0:T(2,128)(2,1)}), bf16[8,2,1536]{2,1,0:T(2,128)(2,1)S(1)}, u32[]{:S(2)}, u32[]{:S(2)}) %all-to-all-start.1) | async-done | bytes 49184 | tf_op jit(solution)/shard_map/all_to_all | solution.py:66
  35.7 7.2 %all_gather.6 = bf16[2,128,512]{1,2,0:T(8,128)(2,1)S(1)} all-gather(bf16[2,128,128]{1,2,0:T(8,128)(2,1)S(1)} %fusion.12), channel_id=1, replica_groups=mesh['tile'=8,'filt'=4] {'filt'}, dimensions={2}, use_global_device_ids=true | all-gather | bytes 327680 | tf_op jit(solution)/shard_map/all_gather | solution.py:92
  43.1 1.7 collective-permute-start
  44.8 1.3 collective-permute-start.1
  46.7 4.3 %collective-permute-done.1 = bf16[2,128,1,128]{3,1,2,0:T(8,128)(2,1)S(1)} collective-permute-done((bf16[2,128,1,128]{3,1,2,0:T(8,128)(2,1)S(1)}, bf16[2,128,1,128]{3,1,2,0:T(8,128)(2,1)S(1)}, u32[]{:S(2)}, u32[]{:S(2)}) %collective-permute-start.1) | collective-permute-done | bytes 65568 | tf_op jit(solution)/shard_map/ppermute | solution.py:21
  53.2 1.1 multiply_convert_fusion
  54.2 5.9 %all_gather.7 = bf16[2,128,4,128]{3,1,2,0:T(8,128)(2,1)S(1)} all-gather(bf16[2,32,4,128]{3,1,2,0:T(8,128)(2,1)S(1)} %get-tuple-element.55), channel_id=1, replica_groups=mesh['tile'=8,'filt'=4] {'filt'}, dimensions={1}, use_global_device_ids=true | all-gather | bytes 327680 | tf_op jit(solution)/shard_map/all_gather | solution.py:108
  62.5 1.3 collective-permute-start.3
  63.8 4.9 %collective-permute-start.2 = (bf16[2,32,1,128]{3,1,2,0:T(8,128)(2,1)S(1)}, bf16[2,32,1,128]{3,1,2,0:T(8,128)(2,1)S(1)}, u32[]{:S(2)}, u32[]{:S(2)}) collective-permute-start(bf16[2,32,1,128]{3,1,2,0:T(8,128)(2,1)S(1)} %get-tuple-element.58), channel_id=1, source_target_pairs={{0,4},{4,8},{8,12},{12,16},{16,20},{20,24},{24,28},{1,5},{5,9},{9,... | collective-permute-start | bytes 49160 | tf_op jit(solution)/shard_map/ppermute | solution.py:19
  69.1 1.1 collective-permute-done.2
  73.2 0.7 copy.418
  74.6 36.8 %psum.23 = f32[3,128,32]{1,2,0:T(8,128)} all-reduce(f32[3,128,32]{1,2,0:T(8,128)S(1)} %maximum_multiply_fusion.1), channel_id=1, replica_groups=mesh['tile'=8,'filt'=4] {'tile'}, use_global_device_ids=true, to_apply=%region_8.9 | all-reduce | flops 12288 | bytes 98304 | tf_op jit(solution)/shard_map/psum | solution.py:190
  111.8 0.7 maximum_multiply_fusion
  112.6 0.9 reshape.92
  114.6 37.0 %psum.21 = f32[12,128]{1,0:T(8,128)} all-reduce(f32[12,128]{1,0:T(8,128)S(1)} %fusion.14), channel_id=1, replica_groups=mesh['tile'=8,'filt'=4] {'tile','filt'}, use_global_device_ids=true, to_apply=%region_6.7 | all-reduce | flops 1536 | bytes 12288 | tf_op jit(solution)/shard_map/psum | solution.py:189
  151.6 28.2 %all-reduce.10.cloned.1.call-done = f32[3,3,128,32]{2,3,1,0:T(8,128)} async-done(((f32[3,3,128,32]{2,3,1,0:T(8,128)}), f32[3,3,128,32]{2,3,1,0:T(8,128)}) %all-reduce.10.cloned.1.call-update) | async-done | bytes 147472 | tf_op jit(solution)/shard_map/psum | solution.py:190
  179.8 1.6 copy.421
  (102 shorter events, 17.0 us)
Async XLA Ops:
  7.2 12.0 %copy-start = (bf16[8,12,128]{2,0,1:T(8,128)(2,1)S(1)}, bf16[8,12,128]{2,0,1:T(8,128)(2,1)}, u32[]{:S(2)}) copy-start(bf16[8,12,128]{2,0,1:T(8,128)(2,1)} %param.7) | copy-start | bytes 73732
  7.2 0.7 copy-start.5
  7.2 9.7 %copy-start.3 = (bf16[3,128,32]{1,2,0:T(8,128)(2,1)S(1)}, bf16[3,128,32]{1,2,0:T(8,128)(2,1)}, u32[]{:S(2)}) copy-start(bf16[3,128,32]{1,2,0:T(8,128)(2,1)} %param.12) | copy-start | bytes 73732
  9.6 13.6 %all-to-all-start = ((s32[8,1,2]{2,1,0:T(1,128)}), s32[8,1,2]{2,1,0:T(1,128)S(1)}, u32[]{:S(2)}, u32[]{:S(2)}) async-start(s32[8,1,2]{2,1,0:T(1,128)} %bitcast.1), calls=%async_computation | async-start | bytes 8192 | tf_op jit(solution)/shard_map/all_to_all | solution.py:73
  16.8 1.1 copy-start.1
  16.8 36.3 %reduce-scatter.5.cloned.1.call-start = ((), (), s32[]{:S(2)}) async-start(), calls=%async_computation.4 | async-start | bytes 327680 | tf_op jit(solution)/shard_map/reduce_scatter | solution.py:142
  23.2 11.1 %all-to-all-start.1 = ((bf16[8,2,1536]{2,1,0:T(2,128)(2,1)}), bf16[8,2,1536]{2,1,0:T(2,128)(2,1)S(1)}, u32[]{:S(2)}, u32[]{:S(2)}) async-start(bf16[8,2,1536]{2,1,0:T(2,128)(2,1)} %reshape.103), calls=%async_computation.1 | async-start | bytes 98304 | tf_op jit(solution)/shard_map/all_to_all | solution.py:66
  27.5 85.0 %reduce-scatter.7.cloned.1.call-start = ((), (), s32[]{:S(2)}) async-start(), calls=%async_computation.6 | async-start | bytes 327680
  34.8 0.7 copy-start.4
  43.1 3.0 %copy-start.2 = (bf16[3,3,128,32]{2,3,1,0:T(8,128)(2,1)S(1)}, bf16[3,3,128,32]{2,3,1,0:T(8,128)(2,1)}, u32[]{:S(2)}) copy-start(bf16[3,3,128,32]{2,3,1,0:T(8,128)(2,1)} %param.11) | copy-start | bytes 221188
  43.1 3.6 %collective-permute-start = (bf16[2,128,1,128]{3,1,2,0:T(8,128)(2,1)S(1)}, bf16[2,128,1,128]{3,1,2,0:T(8,128)(2,1)S(1)}, u32[]{:S(2)}, u32[]{:S(2)}) collective-permute-start(bf16[2,128,1,128]{3,1,2,0:T(8,128)(2,1)S(1)} %get-tuple-element.52), channel_id=1, source_target_pairs={{0,4},{4,8},{8,12},{12,16},{16,20},{20,24},{24,28},{1,5},{5,9},{9,... | collective-permute-start | bytes 196616 | tf_op jit(solution)/shard_map/ppermute | solution.py:19
  44.8 6.2 %collective-permute-start.1 = (bf16[2,128,1,128]{3,1,2,0:T(8,128)(2,1)S(1)}, bf16[2,128,1,128]{3,1,2,0:T(8,128)(2,1)S(1)}, u32[]{:S(2)}, u32[]{:S(2)}) collective-permute-start(bf16[2,128,1,128]{3,1,2,0:T(8,128)(2,1)S(1)} %get-tuple-element.53), channel_id=1, source_target_pairs={{4,0},{8,4},{12,8},{16,12},{20,16},{24,20},{28,24},{5,1},{9,5},{13... | collective-permute-start | bytes 196616 | tf_op jit(solution)/shard_map/ppermute | solution.py:21
  62.5 6.6 %collective-permute-start.3 = (bf16[2,32,1,128]{3,1,2,0:T(8,128)(2,1)S(1)}, bf16[2,32,1,128]{3,1,2,0:T(8,128)(2,1)S(1)}, u32[]{:S(2)}, u32[]{:S(2)}) collective-permute-start(bf16[2,32,1,128]{3,1,2,0:T(8,128)(2,1)S(1)} %get-tuple-element.59), channel_id=1, source_target_pairs={{4,0},{8,4},{12,8},{16,12},{20,16},{24,20},{28,24},{5,1},{9,5},{13... | collective-permute-start | bytes 49160 | tf_op jit(solution)/shard_map/ppermute | solution.py:21
  63.8 6.3 %collective-permute-start.2 = (bf16[2,32,1,128]{3,1,2,0:T(8,128)(2,1)S(1)}, bf16[2,32,1,128]{3,1,2,0:T(8,128)(2,1)S(1)}, u32[]{:S(2)}, u32[]{:S(2)}) collective-permute-start(bf16[2,32,1,128]{3,1,2,0:T(8,128)(2,1)S(1)} %get-tuple-element.58), channel_id=1, source_target_pairs={{0,4},{4,8},{8,12},{12,16},{16,20},{20,24},{24,28},{1,5},{5,9},{9,... | collective-permute-start | bytes 49160 | tf_op jit(solution)/shard_map/ppermute | solution.py:19
  73.9 105.9 %all-reduce.10.cloned.1.call-start = ((), (), s32[]{:S(2)}) async-start(), calls=%async_computation.5 | async-start | bytes 294912 | tf_op jit(solution)/shard_map/psum | solution.py:190
Sparse Core Ops, SparseCore 0:
  20.1 22.7 reduce-scatter.4
  74.0 21.4 reduce-scatter.6
  112.6 67.0 all-reduce.9
where the time goes:
time: 189 us; the launch traced here: 188 us
  blocking collectives  86.8 us (46%)
  waiting for transfers between devices  41.1 us (22%)
  starting transfers between devices  20.9 us (11%)
  between operations  14.2 us (8%)
  matrix products  11.1 us (6%)
  local copies, waits for them, and re-layouts  9.92 us (5%)
  other arithmetic  3.91 us (2%)
    psum x1, blocking collectives, per_device(): grad_stem = lax.psum(stem_part * grad_scale, ('tile', 'filt'))  37 us
    psum x1, blocking collectives, per_device(): lax.psum((spatial_terms * grad_scale, temporal_terms * grad_scale), 'tile')  36.8 us
    psum x1, waiting for transfers between devices, per_device(): lax.psum((spatial_terms * grad_scale, temporal_terms * grad_scale), 'tile')  28.2 us
    all_to_all x1, starting transfers between devices, per_device(): lax.all_to_all(out_dates.reshape(n_tile, CAP), 'tile', split_axis=0, conc...  7.25 us
    all_gather x1, blocking collectives, per_device(): lax.all_gather(feat_quarter, 'filt', axis=2, tiled=True)  7.18 us
    unnamed x22, local copies, waits for them, and re-layouts  6.92 us
    ppermute x2, starting transfers between devices, padded(): lax.ppermute(tail, axis, [(i, (i + 1) % count) for i in range(ends)])  6.6 us
    all_gather x1, blocking collectives, per_device(): act_full = lax.all_gather(activated, 'filt', axis=1, tiled=True)  5.86 us
  transfers between devices with their start and end apart: 9, of which 6 were waited for; matrix products, arithmetic and copies ran while one was open for 7% of the time, Pallas kernels for 0%

commit v1 on v0

v1 whole, which is shorter than its diff:
```python
import functools
import math

import jax
import jax.numpy as jnp
from jax import lax
from jax.experimental import pallas as pl
from jax.experimental.pallas import tpu as pltpu
from jax.sharding import PartitionSpec as P

MESH = pl.DeviceIdType.MESH
F32 = jnp.float32
BF16 = jnp.bfloat16


def loop(count, body):
    if count <= 8:
        for i in range(count):
            body(i)
    else:
        lax.fori_loop(0, count, lambda i, c: (body(i), c)[1], 0)


def total(count, term):
    if count <= 8:
        out = term(0)
        for i in range(1, count):
            out = out + term(i)
        return out
    return lax.fori_loop(1, count, lambda i, c: c + term(i), term(0))


def dot(a, b):
    return jnp.dot(a, b, preferred_element_type=F32)


def dot_t(a, b):
    return lax.dot_general(a, b, (((1,), (1,)), ((), ())), preferred_element_type=F32)


def shifted(block, offset):
    cols = block.shape[1]
    lane = lax.broadcasted_iota(jnp.int32, block.shape, 1)
    if offset == 1:
        return jnp.where(lane == cols - 1, 0.0, pltpu.roll(block, cols - 1, 1))
    return jnp.where(lane == 0, 0.0, pltpu.roll(block, 1, 1))


def kernel(
    n, nf, bp, scale,
    tile_ref, date_ref, panels_ref, stem_ref, wt_ref, cot_ref,
    fo_ref, gstem_ref, gsp_ref, gtm_ref, bg_ref,
    pp, pan_out, pan_in, raw, wall, wback, stem16, stem_t, cot, feat, act, pre_g, pg3,
    rs_out, rs_in, ag, sa_out, sa, sb_out, sb,
    pan_s, pan_r, raw_s, raw_r, w_s, w_r, c_s, c_r, lo_s, lo_r, hi_s, hi_r,
    rs_s, rs_r, ag_s, ag_r, sa_s, sa_r, sb_s, sb_r,
):
    j = lax.axis_index("tile")
    f = lax.axis_index("filt")
    n_slots = panels_ref.shape[0]
    bands = panels_ref.shape[1]
    own = wt_ref.shape[0]
    chan = own * nf
    cols = 128

    def tpeer(d):
        return lax.rem(j + d, n)

    def fpeer(d):
        return lax.rem(f + d, nf)

    def remote(src, dst, s, r, to):
        return pltpu.make_async_remote_copy(
            src_ref=src, dst_ref=dst, send_sem=s, recv_sem=r, device_id=to, device_id_type=MESH
        )

    barrier = pltpu.get_barrier_semaphore()

    def hello(t, g):
        pl.semaphore_signal(barrier, inc=1, device_id=(t, g), device_id_type=MESH)

    loop(n - 1, lambda d: hello(tpeer(d + 1), f))
    for d in range(1, nf):
        hello(j, fpeer(d))

    @pl.when(j > 0)
    def _():
        for d in range(1, nf):
            hello(j - 1, fpeer(d))

    @pl.when(j < n - 1)
    def _():
        for d in range(1, nf):
            hello(j + 1, fpeer(d))

    pad_rows = lax.broadcasted_iota(jnp.int32, (n_slots, 16, cols), 1)
    pp[...] = jnp.where(pad_rows == bands, 1.0, 0.0)
    pp[:, 0:bands, :] = panels_ref[...].astype(F32)

    def fill(k):
        def term(s):
            block = pp[s]
            here = tile_ref[s, 0] == k
            first = jnp.where(here & (date_ref[s] == 0), 1.0, 0.0)
            second = jnp.where(here & (date_ref[s] == 1), 1.0, 0.0)
            return jnp.concatenate([block * first, block * second], axis=0)

        pan_out[k] = total(n_slots, term).astype(BF16)

    loop(n, fill)

    @pl.when(j == 0)
    def _():
        raw[0:2] = jnp.zeros((2, 32, cols), BF16)
        cot[0] = jnp.zeros((2, chan, cols), BF16)

    @pl.when(j == n - 1)
    def _():
        raw[6:8] = jnp.zeros((2, 32, cols), BF16)
        cot[5] = jnp.zeros((2, chan, cols), BF16)

    sides = jnp.where(j > 0, 1, 0) + jnp.where(j < n - 1, 1, 0)
    pl.semaphore_wait(barrier, n - 1 + (nf - 1) * (1 + sides))

    def pan_copy(d):
        k = tpeer(d)
        return remote(pan_out.at[k], pan_in.at[j], pan_s.at[d], pan_r.at[j], (k, f))

    def pan_wait(d):
        k = tpeer(d)
        remote(pan_out.at[k], pan_in.at[k], pan_s.at[d], pan_r.at[k], (k, f)).wait_recv()

    loop(n - 1, lambda d: pan_copy(d + 1).start())

    mine = pl.ds(pl.multiple_of(f * own, own), own)

    def w_copy(d):
        return remote(wt_ref, wall.at[mine], w_s.at[d], w_r.at[f], (j, fpeer(d)))

    def c_copy(d):
        return remote(cot_ref, cot.at[pl.ds(1, 4), :, mine, :], c_s.at[d], c_r.at[f], (j, fpeer(d)))

    def lo_copy(d):
        return remote(cot_ref.at[3], cot.at[0, :, mine, :], lo_s.at[d], lo_r.at[f], (j + 1, fpeer(d)))

    def hi_copy(d):
        return remote(cot_ref.at[0], cot.at[5, :, mine, :], hi_s.at[d], hi_r.at[f], (j - 1, fpeer(d)))

    for d in range(1, nf):
        w_copy(d).start()
    for d in range(1, nf):
        c_copy(d).start()

    @pl.when(j < n - 1)
    def _():
        for d in range(nf):
            lo_copy(d).start()

    @pl.when(j > 0)
    def _():
        for d in range(nf):
            hi_copy(d).start()

    wall[mine, :] = wt_ref[...]
    cot[1:5, :, mine, :] = cot_ref[...]
    stem_t[...] = jnp.zeros((cols, chan), F32)
    stem_t[0:bands, :] = stem_ref[...].astype(F32)
    stem16[...] = stem_t[0:16, :].astype(BF16)
    stem_lhs = stem_t[...].T[:, 0:16].astype(BF16)

    pan_in[j] = pan_out[j]
    loop(n - 1, lambda d: pan_wait(d + 1))
    sums = total(n, lambda k: pan_in[k].astype(F32))
    row = jnp.concatenate(
        [
            sums[t * 16 : t * 16 + 16] / jnp.maximum(sums[t * 16 + bands : t * 16 + bands + 1], 1.0)
            for t in range(2)
        ],
        axis=0,
    ).astype(BF16)
    raw[2 + f] = row

    def raw_copy(d):
        return remote(raw.at[2 + f], raw.at[2 + f], raw_s.at[d], raw_r.at[2 + f], (j, fpeer(d)))

    def raw_down(d):
        return remote(raw.at[2 + f], raw.at[f - 2], raw_s.at[4 + d], raw_r.at[f - 2], (j + 1, fpeer(d)))

    def raw_up(d):
        return remote(raw.at[2 + f], raw.at[6 + f], raw_s.at[4 + d], raw_r.at[6 + f], (j - 1, fpeer(d)))

    for d in range(1, nf):
        raw_copy(d).start()
    goes_down = (f >= 2) & (j < n - 1)
    goes_up = (f < 2) & (j > 0)

    @pl.when(goes_down)
    def _():
        for d in range(nf):
            raw_down(d).start()

    @pl.when(goes_up)
    def _():
        for d in range(nf):
            raw_up(d).start()

    for d in range(1, nf):
        g = fpeer(d)
        theirs = pl.ds(pl.multiple_of(g * own, own), own)
        remote(wt_ref, wall.at[theirs], w_s.at[d], w_r.at[g], (j, g)).wait_recv()
    for q in range(12):
        block = wall[:, q * chan : (q + 1) * chan].astype(F32).T.astype(BF16)
        at = q if q < 9 else 9 + (11 - q)
        wback[:, at * chan : (at + 1) * chan] = block

    def raw_wait(slot):
        remote(raw.at[slot], raw.at[slot], raw_s.at[0], raw_r.at[slot], (j, fpeer(1))).wait_recv()

    for d in range(1, nf):
        raw_wait(2 + fpeer(d))

    @pl.when(j > 0)
    def _():
        raw_wait(0)
        raw_wait(1)

    @pl.when(j < n - 1)
    def _():
        raw_wait(6)
        raw_wait(7)

    for t in range(2):
        for r in range(8):
            block = dot(stem_lhs, raw[r, t * 16 : t * 16 + 16, :]).astype(BF16)
            at = (t * 8 + r) * cols
            wide = block.astype(F32)
            feat[0:chan, at : at + cols] = shifted(wide, -1).astype(BF16)
            feat[chan : 2 * chan, at : at + cols] = block
            feat[2 * chan : 3 * chan, at : at + cols] = shifted(wide, 1).astype(BF16)

    for d in range(1, nf):
        g = fpeer(d)
        theirs = pl.ds(pl.multiple_of(g * own, own), own)
        remote(cot_ref, cot.at[pl.ds(1, 4), :, theirs, :], c_s.at[d], c_r.at[g], (j, g)).wait_recv()

    @pl.when(j > 0)
    def _():
        for g in range(nf):
            remote(cot_ref.at[3], cot.at[0, :, g * own : (g + 1) * own, :], lo_s.at[g], lo_r.at[g], (j - 1, g)).wait_recv()

    @pl.when(j < n - 1)
    def _():
        for g in range(nf):
            remote(cot_ref.at[0], cot.at[5, :, g * own : (g + 1) * own, :], hi_s.at[g], hi_r.at[g], (j + 1, g)).wait_recv()

    cot_rows = jnp.concatenate([cot[r].reshape(2 * chan, cols) for r in range(6)], axis=1)
    lane = lax.broadcasted_iota(jnp.int32, (chan, 6 * cols), 1)
    inside = ((lane >= cols) | (j > 0)) & ((lane < 5 * cols) | (j < n - 1))
    for t in range(2):
        pre = dot(wall[:, 0 : 3 * chan], feat[:, t * 1024 : t * 1024 + 768])
        for dy in (1, 2):
            at = t * 1024 + dy * cols
            pre = pre + dot(wall[:, dy * 3 * chan : (dy + 1) * 3 * chan], feat[:, at : at + 768])
        sigma = jax.nn.sigmoid(pre)
        act[t * chan : (t + 1) * chan, :] = (pre * sigma)[:, cols : 5 * cols].astype(BF16)
        act_grad = dot(wback[:, (10 - t) * chan : (12 - t) * chan], cot_rows)
        slope = sigma * (1.0 + pre * (1.0 - sigma))
        pre_g[:, t * 768 : (t + 1) * 768] = jnp.where(inside, act_grad * slope, 0.0).astype(BF16)

    def put(q, grad):
        for h in range(2):
            b = q * 2 + h
            rs_out[b // bp, (b % bp) * 16 : (b % bp) * 16 + 16, :] = grad[h * 16 : h * 16 + 16].astype(BF16)

    cot_own = [
        jnp.concatenate([cot_ref[r, t] for r in range(4)], axis=1) for t in range(2)
    ]
    act0, act1 = act[0:chan, :], act[chan : 2 * chan, :]
    put(9, dot_t(cot_own[1], act0) * scale)
    put(10, (dot_t(cot_own[0], act0) + dot_t(cot_own[1], act1)) * scale)
    put(11, dot_t(cot_own[0], act1) * scale)
    pg_own = [pre_g[mine, t * 768 + cols : t * 768 + 5 * cols] for t in range(2)]
    for dy in range(3):
        at = (dy + 1) * cols
        grad = dot_t(pg_own[0], feat[:, at : at + 512])
        grad = grad + dot_t(pg_own[1], feat[:, 1024 + at : 1024 + at + 512])
        grad = grad * scale
        for dx in range(3):
            put(dy * 3 + dx, grad[:, dx * chan : (dx + 1) * chan])
    if n * bp > 24:
        used = -(-24 // bp)
        loop(n - used, lambda k: rs_out.__setitem__(used + k, jnp.zeros((bp * 16, cols), BF16)))

    def rs_copy(d):
        k = tpeer(d)
        return remote(rs_out.at[k], rs_in.at[j], rs_s.at[d], rs_r.at[j], (k, f))

    loop(n - 1, lambda d: rs_copy(d + 1).start())
    rs_in[j] = rs_out[j]

    for t in range(2):
        for r in range(3):
            at = pl.ds(pl.multiple_of(t * 768 + (f + r) * cols, cols), cols)
            block = pre_g[:, at]
            wide = block.astype(F32)
            to = (r * 2 + t) * cols
            pg3[0:chan, to : to + cols] = shifted(wide, 1).astype(BF16)
            pg3[chan : 2 * chan, to : to + cols] = block
            pg3[2 * chan : 3 * chan, to : to + cols] = shifted(wide, -1).astype(BF16)
    fgrad = jnp.concatenate([cot[1 + f, t].astype(F32) for t in range(2)], axis=1)
    for dy in range(3):
        at = (2 - dy) * 2 * cols
        fgrad = fgrad + dot(wback[:, dy * 3 * chan : (dy + 1) * 3 * chan], pg3[:, at : at + 2 * cols])
    upper = fgrad.astype(BF16)
    lower = (fgrad - upper.astype(F32)).astype(BF16)
    own_raw = raw[2 + f]
    raw_row = jnp.concatenate([own_raw[0:16], own_raw[16:32]], axis=1)
    sa_out[...] = (dot_t(raw_row, upper) + dot_t(raw_row, lower)) * scale

    def sa_copy(d):
        return remote(sa_out, sa.at[f], sa_s.at[d], sa_r.at[f], (j, fpeer(d)))

    for d in range(1, nf):
        sa_copy(d).start()
    sa[f] = sa_out[...]
    bgrad = dot(stem16[...], upper) + dot(stem16[...], lower)
    for t in range(2):
        bg_ref[t] = bgrad[0:bands, t * cols : (t + 1) * cols]

    wt_time = wt_ref[:, 9 * chan : 12 * chan]
    feat_own = pl.ds(pl.multiple_of(chan + f * own, own), own)
    for t in range(2):
        out = dot(wt_time[:, (1 - t) * chan : (3 - t) * chan], act[...])
        out = out + feat[feat_own, t * 1024 + 256 : t * 1024 + 768].astype(F32)
        for r in range(4):
            fo_ref[t, r] = out[:, r * cols : (r + 1) * cols].astype(BF16)

    for d in range(1, nf):
        g = fpeer(d)
        remote(sa_out, sa.at[g], sa_s.at[d], sa_r.at[g], (j, g)).wait_recv()
    sb_out[...] = (sa[0] + sa[1]) + (sa[2] + sa[3])

    def sb_copy(d):
        k = tpeer(d)
        return remote(sb_out, sb.at[j], sb_s.at[d], sb_r.at[j], (k, f))

    loop(n - 1, lambda d: sb_copy(d + 1).start())
    sb[j] = sb_out[...]

    def rs_wait(d):
        k = tpeer(d)
        remote(rs_out.at[k], rs_in.at[k], rs_s.at[d], rs_r.at[k], (k, f)).wait_recv()

    loop(n - 1, lambda d: rs_wait(d + 1))
    ag[j] = total(n, lambda k: rs_in[k].astype(F32)).astype(BF16)

    def ag_copy(d):
        k = tpeer(d)
        return remote(ag.at[j], ag.at[j], ag_s.at[d], ag_r.at[j], (k, f))

    loop(n - 1, lambda d: ag_copy(d + 1).start())

    loop(n - 1, lambda d: pan_copy(d + 1).wait_send())
    for d in range(1, nf):
        w_copy(d).wait_send()
        c_copy(d).wait_send()
        raw_copy(d).wait_send()
        sa_copy(d).wait_send()

    @pl.when(j < n - 1)
    def _():
        for d in range(nf):
            lo_copy(d).wait_send()

    @pl.when(j > 0)
    def _():
        for d in range(nf):
            hi_copy(d).wait_send()

    @pl.when(goes_down)
    def _():
        for d in range(nf):
            raw_down(d).wait_send()

    @pl.when(goes_up)
    def _():
        for d in range(nf):
            raw_up(d).wait_send()

    loop(n - 1, lambda d: rs_copy(d + 1).wait_send())

    def sb_wait(d):
        k = tpeer(d)
        remote(sb_out, sb.at[k], sb_s.at[d], sb_r.at[k], (k, f)).wait_recv()

    loop(n - 1, lambda d: sb_wait(d + 1))
    gstem_ref[...] = total(n, lambda k: sb[k])[0:bands]

    def ag_wait(d):
        k = tpeer(d)
        remote(ag.at[k], ag.at[k], ag_s.at[d], ag_r.at[k], (k, f)).wait_recv()

    loop(n - 1, lambda d: ag_wait(d + 1))
    for q in range(12):
        halves = []
        for h in range(2):
            b = q * 2 + h
            halves.append(ag[b // bp, (b % bp) * 16 : (b % bp) * 16 + 16, :].astype(F32))
        block = jnp.concatenate(halves, axis=0).T
        if q < 9:
            gsp_ref[q] = block
        else:
            gtm_ref[q - 9] = block
    loop(n - 1, lambda d: ag_copy(d + 1).wait_send())
    loop(n - 1, lambda d: sb_copy(d + 1).wait_send())


def per_device(
    panels, panel_tile, panel_date, stem_weight, spatial_weight, temporal_weight, cotangent
):
    n = lax.axis_size("tile")
    nf = lax.axis_size("filt")
    n_slots, n_bands, cols = panels.shape
    n_dates, own, n_rows, _ = cotangent.shape
    chan = stem_weight.shape[1]
    bp = -(-24 // n)
    scale = 1.0 / math.sqrt(n_dates * n_rows * n * cols)
    weights = jnp.concatenate([spatial_weight.reshape(9, chan, own), temporal_weight], axis=0)
    wt = weights.transpose(2, 0, 1).reshape(own, 12 * chan)
    cot = cotangent.transpose(2, 0, 1, 3)
    dma = pltpu.SemaphoreType.DMA
    vmem = pl.BlockSpec(memory_space=pltpu.VMEM)
    smem = pl.BlockSpec(memory_space=pltpu.SMEM)
    out = pl.pallas_call(
        functools.partial(kernel, n, nf, bp, scale),
        out_shape=(
            jax.ShapeDtypeStruct((n_dates, n_rows, own, cols), BF16),
            jax.ShapeDtypeStruct((n_bands, chan), F32),
            jax.ShapeDtypeStruct((9, chan, own), F32),
            jax.ShapeDtypeStruct((3, chan, own), F32),
            jax.ShapeDtypeStruct((n_dates, n_bands, cols), F32),
        ),
        in_specs=[smem, smem, vmem, vmem, vmem, vmem],
        out_specs=(vmem,) * 5,
        scratch_shapes=[
            pltpu.VMEM((n_slots, 16, cols), F32),
            pltpu.VMEM((n, 32, cols), BF16),
            pltpu.VMEM((n, 32, cols), BF16),
            pltpu.VMEM((8, 32, cols), BF16),
            pltpu.VMEM((chan, 12 * chan), BF16),
            pltpu.VMEM((chan, 12 * chan), BF16),
            pltpu.VMEM((16, chan), BF16),
            pltpu.VMEM((cols, chan), F32),
            pltpu.VMEM((6, 2, chan, cols), BF16),
            pltpu.VMEM((3 * chan, 2 * 8 * cols), BF16),
            pltpu.VMEM((2 * chan, 4 * cols), BF16),
            pltpu.VMEM((chan, 2 * 6 * cols), BF16),
            pltpu.VMEM((3 * chan, 6 * cols), BF16),
            pltpu.VMEM((n, bp * 16, cols), BF16),
            pltpu.VMEM((n, bp * 16, cols), BF16),
            pltpu.VMEM((n, bp * 16, cols), BF16),
            pltpu.VMEM((16, cols), F32),
            pltpu.VMEM((nf, 16, cols), F32),
            pltpu.VMEM((16, cols), F32),
            pltpu.VMEM((n, 16, cols), F32),
            dma((n,)), dma((n,)), dma((8,)), dma((8,)), dma((nf,)), dma((nf,)),
            dma((nf,)), dma((nf,)), dma((nf,)), dma((nf,)), dma((nf,)), dma((nf,)),
            dma((n,)), dma((n,)), dma((n,)), dma((n,)), dma((nf,)), dma((nf,)), dma((n,)), dma((n,)),
        ],
        compiler_params=pltpu.CompilerParams(
            collective_id=0, has_side_effects=True, vmem_limit_bytes=40 * 1024 * 1024
        ),
    )(panel_tile, panel_date, panels, stem_weight, wt, cot)
    features_out, grad_stem, grad_spatial, grad_temporal, band_grad = out
    return (
        features_out.transpose(0, 2, 1, 3),
        grad_stem,
        grad_spatial.reshape(3, 3, chan, own),
        grad_temporal,
        band_grad,
    )


def solution(mesh):
    in_specs = (
        P("tile", None, "filt"),
        P("tile", None),
        P("tile"),
        P(),
        P(None, None, None, "filt"),
        P(None, None, "filt"),
        P(None, "filt", "tile", None),
    )
    out_specs = (
        P(None, "filt", "tile", None),
        P(),
        P(None, None, None, "filt"),
        P(None, None, "filt"),
        P(None, None, ("tile", "filt")),
    )
    return jax.shard_map(
        per_device, mesh=mesh, in_specs=in_specs, out_specs=out_specs, check_vma=False
    )
```

time: 189 us -> 38.2 us (0.20)
  blocking collectives: 86.8 us -> 0 us
  waiting for transfers between devices: 41.1 us -> 0 us
  Pallas kernels: 0 us -> 29.8 us
  starting transfers between devices: 20.9 us -> 0 us
  between operations: 14.2 us -> 0.71 us
  matrix products: 11.1 us -> 0 us
  other arithmetic: 3.91 us -> 0.05 us
  local copies, waits for them, and re-layouts: 9.92 us -> 7.32 us
    psum x2 -> x0, blocking collectives: 73.8 us -> none  [the longest x1 37 us: per_device(): grad_stem = lax.psum(stem_part * grad_scale, ('tile', 'filt'))]
    pallas_call x0 -> x1, Pallas kernels: none -> 29.8 us  [per_device(): pl.pallas_call(functools.partial(kernel, n, nf, bp, scale), out_shape=(ja...]
    psum x1 -> x0, waiting for transfers between devices: 28.2 us -> none  [per_device(): lax.psum((spatial_terms * grad_scale, temporal_terms * grad_scale), 'tile')]
    all_gather x2 -> x0, blocking collectives: 13 us -> none  [the longest x1 7.18 us: per_device(): lax.all_gather(feat_quarter, 'filt', axis=2, tiled=True)]
    all_to_all x2 -> x0, starting transfers between devices: 11.6 us -> none  [the longest x1 7.25 us: per_device(): lax.all_to_all(out_dates.reshape(n_tile, CAP), 'tile', split_axis=0, conc...]
    dot_general x42 -> x0, matrix products: 11.1 us -> none  [the longest x9 2.67 us: per_device(): jnp.einsum('tirw,io->torw', shifted[col_off][:, :, row_off:row_off + n_ro...]
    ppermute x4 -> x0, starting transfers between devices: 9.21 us -> none  [the longest x2 6.6 us: padded(): lax.ppermute(tail, axis, [(i, (i + 1) % count) for i in range(ends)])]
    all_to_all x2 -> x0, waiting for transfers between devices: 7.04 us -> none  [the longest x1 5.36 us: per_device(): lax.all_to_all(outgoing.reshape(n_tile, CAP * n_bands * quarter), 'tile',...]
  transfers between devices with their start and end apart: 9 -> 0, of which waited for: 6 -> 0; matrix products, arithmetic and copies ran while one was open for 7% -> 0% of each run, Pallas kernels for 0% -> 0%
where the time goes in v1:
time: 38.2 us; the launch traced here: 37.9 us
  Pallas kernels  29.8 us (78%)
  local copies, waits for them, and re-layouts  7.32 us (19%)
  between operations  0.71 us (2%)
    pallas_call x1, Pallas kernels, per_device(): pl.pallas_call(functools.partial(kernel, n, nf, bp, scale), out_shape=(ja...  29.8 us
    unnamed x18, local copies, waits for them, and re-layouts  7.28 us

profile of v1, /device:TPU:0, one launch (start us, length us, event | category | flops | bytes accessed | tf_op | source)
XLA Modules:
  0.0 37.9 jit_solution(1519872079069167814)
XLA Ops:
  0.6 0.0 copy-start.3
  0.6 0.8 %copy.24.tile_ref = s32[8,1]{1,0:T(8,128)S(1)} copy(s32[8,1]{0,1:T(1,128)} %param.8) | data formatting | bytes 64 | tf_op args[1]
  1.4 0.7 %copy.25.panels_ref = bf16[8,12,128]{2,1,0:T(8,128)(2,1)S(1)} copy(bf16[8,12,128]{2,0,1:T(8,128)(2,1)} %param.7) | data formatting | bytes 49152 | tf_op args[0]
  2.1 0.8 %copy.22 = bf16[3,128,32]{1,0,2:T(4,128)(2,1)S(1)} copy(bf16[3,128,32]{1,2,0:T(8,128)(2,1)} %param.12) | data formatting | bytes 49152 | tf_op args[5]
  2.9 0.0 copy-done.3
  2.9 0.0 copy-start.2
  2.9 0.9 %copy-done.2 = bf16[3,3,128,32]{2,3,1,0:T(8,128)(2,1)S(1)} copy-done((bf16[3,3,128,32]{2,3,1,0:T(8,128)(2,1)S(1)}, bf16[3,3,128,32]{2,3,1,0:T(8,128)(2,1)}, u32[]{:S(2)}) %copy-start.2) | copy-done | bytes 73752
  3.8 0.1 pad_maximum_fusion
  3.9 0.0 copy-start
  4.0 0.0 copy-start.1
  4.0 0.6 %copy-done = bf16[12,128]{1,0:T(8,128)(2,1)S(1)} copy-done((bf16[12,128]{1,0:T(8,128)(2,1)S(1)}, bf16[12,128]{1,0:T(8,128)(2,1)}, u32[]{:S(2)}) %copy-start) | copy-done | bytes 3096
  4.6 0.0 copy-done.1
  4.6 29.8 %shard_map.110 = (bf16[2,4,32,128]{3,2,1,0:T(8,128)(2,1)S(1)}, f32[12,128]{1,0:T(8,128)S(1)}, f32[9,128,32]{2,1,0:T(8,128)S(1)}, f32[3,128,32]{2,1,0:T(8,128)S(1)}, f32[2,12,128]{2,1,0:T(8,128)S(1)}) custom-call(s32[8,1]{1,0:T(8,128)S(1)} %copy.24.tile_ref, s32[8]{0:T(128)S(1)} %copy-done.1, bf16[8,12,128]{2,1,0:T(8,128)(2,1)S(1)} %copy.25.panels_ref, ...), custom_call_target="tpu_custom_call" | custom-call | tf_op jit(solution)/shard_map/pallas_call | solution.py:434
  34.4 0.7 %copy.26 = bf16[2,32,4,128]{3,2,1,0:T(4,128)(2,1)} copy(bf16[2,32,4,128]{3,1,2,0:T(8,128)(2,1)S(1)} %bitcast.14) | data formatting | bytes 131072
  35.1 0.6 %copy.29 = f32[2,12,128]{2,0,1:T(2,128)} copy(f32[2,12,128]{2,1,0:T(8,128)S(1)} %get-tuple-element.24) | data formatting | bytes 24576
  35.7 0.7 %copy.28 = f32[3,128,32]{1,2,0:T(8,128)} copy(f32[3,128,32]{2,1,0:T(8,128)S(1)} %get-tuple-element.23) | data formatting | bytes 98304
  36.4 0.9 %copy.27 = f32[3,3,128,32]{2,3,1,0:T(8,128)} copy(f32[3,3,128,32]{3,2,1,0:T(8,128)S(1)} %bitcast.11) | data formatting | bytes 294912
  37.3 0.6 %copy.36 = f32[12,128]{1,0:T(8,128)} copy(f32[12,128]{1,0:T(8,128)S(1)} %get-tuple-element.31) | data formatting | bytes 12288
  (3 shorter events, 0.1 us)
Async XLA Ops:
  0.6 2.3 %copy-start.3 = (bf16[2,32,4,128]{3,2,1,0:T(4,128)(2,1)S(1)}, bf16[2,32,4,128]{3,2,1,0:T(4,128)(2,1)}, u32[]{:S(2)}) copy-start(bf16[2,32,4,128]{3,2,1,0:T(4,128)(2,1)} %param.13) | copy-start | bytes 196612
  2.9 0.9 %copy-start.2 = (bf16[3,3,128,32]{2,3,1,0:T(8,128)(2,1)S(1)}, bf16[3,3,128,32]{2,3,1,0:T(8,128)(2,1)}, u32[]{:S(2)}) copy-start(bf16[3,3,128,32]{2,3,1,0:T(8,128)(2,1)} %param.11) | copy-start | bytes 221188
  3.9 0.7 %copy-start = (bf16[12,128]{1,0:T(8,128)(2,1)S(1)}, bf16[12,128]{1,0:T(8,128)(2,1)}, u32[]{:S(2)}) copy-start(bf16[12,128]{1,0:T(8,128)(2,1)} %stem_ref.1) | copy-start | bytes 9220
  4.0 0.7 %copy-start.1 = (s32[8]{0:T(128)S(1)}, s32[8]{0:T(128)}, u32[]{:S(2)}) copy-start(s32[8]{0:T(128)} %date_ref.1) | copy-start | bytes 100

commit v2 on v1

--- a/solution.py
+++ b/solution.py
@@ -48,8 +48,8 @@
 
 def kernel(
     n, nf, bp, scale,
-    tile_ref, date_ref, panels_ref, stem_ref, wt_ref, cot_ref,
-    fo_ref, gstem_ref, gsp_ref, gtm_ref, bg_ref,
+    tile_ref, date_ref, panels_ref, stem_ref, ws_ref, wtm_ref, cot_ref,
+    fo_ref, gstem_ref, grad_ref, bg_ref,
     pp, pan_out, pan_in, raw, wall, wback, stem16, stem_t, cot, feat, act, pre_g, pg3,
     rs_out, rs_in, ag, sa_out, sa, sb_out, sb,
     pan_s, pan_r, raw_s, raw_r, w_s, w_r, c_s, c_r, lo_s, lo_r, hi_s, hi_r,
@@ -57,9 +57,8 @@
 ):
     j = lax.axis_index("tile")
     f = lax.axis_index("filt")
-    n_slots = panels_ref.shape[0]
-    bands = panels_ref.shape[1]
-    own = wt_ref.shape[0]
+    bands, n_slots = panels_ref.shape[0:2]
+    own = ws_ref.shape[1]
     chan = own * nf
     cols = 128
 
@@ -93,14 +92,18 @@
         for d in range(1, nf):
             hello(j + 1, fpeer(d))
 
+    mine = pl.ds(pl.multiple_of(f * own, own), own)
+    for q in range(12):
+        wall[mine, q * chan : (q + 1) * chan] = ws_ref[q] if q < 9 else wtm_ref[q - 9]
     pad_rows = lax.broadcasted_iota(jnp.int32, (n_slots, 16, cols), 1)
     pp[...] = jnp.where(pad_rows == bands, 1.0, 0.0)
-    pp[:, 0:bands, :] = panels_ref[...].astype(F32)
+    for b in range(bands):
+        pp[:, b, :] = panels_ref[b].astype(F32)
 
     def fill(k):
         def term(s):
             block = pp[s]
-            here = tile_ref[s, 0] == k
+            here = tile_ref[0, s] == k
             first = jnp.where(here & (date_ref[s] == 0), 1.0, 0.0)
             second = jnp.where(here & (date_ref[s] == 1), 1.0, 0.0)
             return jnp.concatenate([block * first, block * second], axis=0)
@@ -132,13 +135,33 @@
 
     loop(n - 1, lambda d: pan_copy(d + 1).start())
 
-    mine = pl.ds(pl.multiple_of(f * own, own), own)
-
-    def w_copy(d):
-        return remote(wt_ref, wall.at[mine], w_s.at[d], w_r.at[f], (j, fpeer(d)))
-
-    def c_copy(d):
-        return remote(cot_ref, cot.at[pl.ds(1, 4), :, mine, :], c_s.at[d], c_r.at[f], (j, fpeer(d)))
+    sib = f + 1 - 2 * lax.rem(f, 2)
+    par = lax.rem(f + 2, nf)
+    diag = lax.rem(sib + 2, nf)
+
+    def group(g):
+        return pl.ds(pl.multiple_of(g * own, own), own)
+
+    def w_copy(to, slot):
+        return remote(wall.at[mine], wall.at[mine], w_s.at[slot], w_r.at[f], (j, to))
+
+    def c_copy(to, slot):
+        return remote(cot_ref, cot.at[pl.ds(1, 4), :, mine, :], c_s.at[slot], c_r.at[f], (j, to))
+
+    def w_forward():
+        at = wall.at[group(par)]
+        return remote(at, at, w_s.at[2], w_r.at[par], (j, sib))
+
+    def c_forward():
+        at = cot.at[pl.ds(1, 4), :, group(par), :]
+        return remote(at, at, c_s.at[2], c_r.at[par], (j, sib))
+
+    def w_wait(g):
+        remote(wall.at[mine], wall.at[group(g)], w_s.at[0], w_r.at[g], (j, par)).wait_recv()
+
+    def c_wait(g):
+        at = cot.at[pl.ds(1, 4), :, group(g), :]
+        remote(cot_ref, at, c_s.at[0], c_r.at[g], (j, par)).wait_recv()
 
     def lo_copy(d):
         return remote(cot_ref.at[3], cot.at[0, :, mine, :], lo_s.at[d], lo_r.at[f], (j + 1, fpeer(d)))
@@ -146,10 +169,10 @@
     def hi_copy(d):
         return remote(cot_ref.at[0], cot.at[5, :, mine, :], hi_s.at[d], hi_r.at[f], (j - 1, fpeer(d)))
 
-    for d in range(1, nf):
-        w_copy(d).start()
-    for d in range(1, nf):
-        c_copy(d).start()
+    w_copy(par, 0).start()
+    w_copy(sib, 1).start()
+    c_copy(par, 0).start()
+    c_copy(sib, 1).start()
 
     @pl.when(j < n - 1)
     def _():
@@ -161,7 +184,6 @@
         for d in range(nf):
             hi_copy(d).start()
 
-    wall[mine, :] = wt_ref[...]
     cot[1:5, :, mine, :] = cot_ref[...]
     stem_t[...] = jnp.zeros((cols, chan), F32)
     stem_t[0:bands, :] = stem_ref[...].astype(F32)
@@ -204,14 +226,8 @@
         for d in range(nf):
             raw_up(d).start()
 
-    for d in range(1, nf):
-        g = fpeer(d)
-        theirs = pl.ds(pl.multiple_of(g * own, own), own)
-        remote(wt_ref, wall.at[theirs], w_s.at[d], w_r.at[g], (j, g)).wait_recv()
-    for q in range(12):
-        block = wall[:, q * chan : (q + 1) * chan].astype(F32).T.astype(BF16)
-        at = q if q < 9 else 9 + (11 - q)
-        wback[:, at * chan : (at + 1) * chan] = block
+    w_wait(par)
+    w_forward().start()
 
     def raw_wait(slot):
         remote(raw.at[slot], raw.at[slot], raw_s.at[0], raw_r.at[slot], (j, fpeer(1))).wait_recv()
@@ -238,10 +254,16 @@
             feat[chan : 2 * chan, at : at + cols] = block
             feat[2 * chan : 3 * chan, at : at + cols] = shifted(wide, 1).astype(BF16)
 
-    for d in range(1, nf):
-        g = fpeer(d)
-        theirs = pl.ds(pl.multiple_of(g * own, own), own)
-        remote(cot_ref, cot.at[pl.ds(1, 4), :, theirs, :], c_s.at[d], c_r.at[g], (j, g)).wait_recv()
+    c_wait(par)
+    c_forward().start()
+    w_wait(sib)
+    w_wait(diag)
+    for q in range(12):
+        block = wall[:, q * chan : (q + 1) * chan].astype(F32).T.astype(BF16)
+        at = q if q < 9 else 9 + (11 - q)
+        wback[:, at * chan : (at + 1) * chan] = block
+    c_wait(sib)
+    c_wait(diag)
 
     @pl.when(j > 0)
     def _():
@@ -327,7 +349,7 @@
     for t in range(2):
         bg_ref[t] = bgrad[0:bands, t * cols : (t + 1) * cols]
 
-    wt_time = wt_ref[:, 9 * chan : 12 * chan]
+    wt_time = wall[mine, 9 * chan : 12 * chan]
     feat_own = pl.ds(pl.multiple_of(chan + f * own, own), own)
     for t in range(2):
         out = dot(wt_time[:, (1 - t) * chan : (3 - t) * chan], act[...])
@@ -360,10 +382,14 @@
 
     loop(n - 1, lambda d: ag_copy(d + 1).start())
 
+    w_copy(par, 0).wait_send()
+    w_copy(sib, 1).wait_send()
+    w_forward().wait_send()
+    c_copy(par, 0).wait_send()
+    c_copy(sib, 1).wait_send()
+    c_forward().wait_send()
     loop(n - 1, lambda d: pan_copy(d + 1).wait_send())
     for d in range(1, nf):
-        w_copy(d).wait_send()
-        c_copy(d).wait_send()
         raw_copy(d).wait_send()
         sa_copy(d).wait_send()
 
@@ -401,18 +427,25 @@
         remote(ag.at[k], ag.at[k], ag_s.at[d], ag_r.at[k], (k, f)).wait_recv()
 
     loop(n - 1, lambda d: ag_wait(d + 1))
-    for q in range(12):
-        halves = []
-        for h in range(2):
-            b = q * 2 + h
-            halves.append(ag[b // bp, (b % bp) * 16 : (b % bp) * 16 + 16, :].astype(F32))
-        block = jnp.concatenate(halves, axis=0).T
-        if q < 9:
-            gsp_ref[q] = block
-        else:
-            gtm_ref[q - 9] = block
+    for b in range(24):
+        grad_ref[b] = ag[b // bp, (b % bp) * 16 : (b % bp) * 16 + 16, :]
     loop(n - 1, lambda d: ag_copy(d + 1).wait_send())
     loop(n - 1, lambda d: sb_copy(d + 1).wait_send())
+
+
+def finish(fo_in, gstem_in, grad_in, bg_in, fo_ref, gstem_ref, gsp_ref, gtm_ref, bg_ref):
+    for t in range(2):
+        fo_ref[t] = jnp.swapaxes(fo_in[t].astype(F32), 0, 1).astype(BF16)
+    gstem_ref[...] = gstem_in[...]
+    for t in range(2):
+        bg_ref[:, t, :] = bg_in[t]
+    for q in range(12):
+        for h in range(2):
+            block = grad_in[2 * q + h].astype(F32)
+            if q < 9:
+                gsp_ref[q, h * 16 : h * 16 + 16, :] = block
+            else:
+                gtm_ref[q - 9, h * 16 : h * 16 + 16, :] = block
 
 
 def per_device(
@@ -425,8 +458,8 @@
     chan = stem_weight.shape[1]
     bp = -(-24 // n)
     scale = 1.0 / math.sqrt(n_dates * n_rows * n * cols)
-    weights = jnp.concatenate([spatial_weight.reshape(9, chan, own), temporal_weight], axis=0)
-    wt = weights.transpose(2, 0, 1).reshape(own, 12 * chan)
+    ws = spatial_weight.transpose(0, 1, 3, 2).reshape(9, own, chan)
+    wtm = temporal_weight.transpose(0, 2, 1)
     cot = cotangent.transpose(2, 0, 1, 3)
     dma = pltpu.SemaphoreType.DMA
     vmem = pl.BlockSpec(memory_space=pltpu.VMEM)
@@ -436,12 +469,11 @@
         out_shape=(
             jax.ShapeDtypeStruct((n_dates, n_rows, own, cols), BF16),
             jax.ShapeDtypeStruct((n_bands, chan), F32),
-            jax.ShapeDtypeStruct((9, chan, own), F32),
-            jax.ShapeDtypeStruct((3, chan, own), F32),
+            jax.ShapeDtypeStruct((24, 16, cols), BF16),
             jax.ShapeDtypeStruct((n_dates, n_bands, cols), F32),
         ),
-        in_specs=[smem, smem, vmem, vmem, vmem, vmem],
-        out_specs=(vmem,) * 5,
+        in_specs=[smem, smem, vmem, vmem, vmem, vmem, vmem],
+        out_specs=(vmem,) * 4,
         scratch_shapes=[
             pltpu.VMEM((n_slots, 16, cols), F32),
             pltpu.VMEM((n, 32, cols), BF16),
@@ -470,14 +502,25 @@
         compiler_params=pltpu.CompilerParams(
             collective_id=0, has_side_effects=True, vmem_limit_bytes=40 * 1024 * 1024
         ),
-    )(panel_tile, panel_date, panels, stem_weight, wt, cot)
-    features_out, grad_stem, grad_spatial, grad_temporal, band_grad = out
+    )(panel_tile.T, panel_date, panels.transpose(1, 0, 2), stem_weight, ws, wtm, cot)
+    features_out, grad_stem, gsp, gtm, bg = pl.pallas_call(
+        finish,
+        out_shape=(
+            jax.ShapeDtypeStruct((n_dates, own, n_rows, cols), BF16),
+            jax.ShapeDtypeStruct((n_bands, chan), F32),
+            jax.ShapeDtypeStruct((9, own, chan), F32),
+            jax.ShapeDtypeStruct((3, own, chan), F32),
+            jax.ShapeDtypeStruct((n_bands, n_dates, cols), F32),
+        ),
+        in_specs=[vmem] * 4,
+        out_specs=(vmem,) * 5,
+    )(*out)
     return (
-        features_out.transpose(0, 2, 1, 3),
+        features_out,
         grad_stem,
-        grad_spatial.reshape(3, 3, chan, own),
-        grad_temporal,
-        band_grad,
+        gsp.reshape(3, 3, own, chan).transpose(0, 1, 3, 2),
+        gtm.transpose(0, 2, 1),
+        bg.transpose(1, 0, 2),
     )
 
 

time: 38.2 us -> 34.2 us (0.90)
  local copies, waits for them, and re-layouts: 7.32 us -> 3.98 us
  Pallas kernels: 29.8 us -> 29.3 us
    unnamed x18 -> x21, local copies, waits for them, and re-layouts: 7.28 us -> 3.98 us
    pallas_call x1, Pallas kernels: 29.8 us -> 27.6 us  [per_device(): pl.pallas_call(functools.partial(kernel, n, nf, bp, scale), out_shape=(ja...]
    pallas_call x0 -> x1, Pallas kernels: none -> 1.68 us  [per_device(): pl.pallas_call(finish, out_shape=(jax.ShapeDtypeStruct((n_dates, own, n_r...]
where the time goes in v2:
time: 34.2 us; the launch traced here: 34 us
  Pallas kernels  29.3 us (86%)
  local copies, waits for them, and re-layouts  3.98 us (12%)
  between operations  0.74 us (2%)
    pallas_call x1, Pallas kernels, per_device(): pl.pallas_call(functools.partial(kernel, n, nf, bp, scale), out_shape=(ja...  27.6 us
    unnamed x21, local copies, waits for them, and re-layouts  3.98 us
    pallas_call x1, Pallas kernels, per_device(): pl.pallas_call(finish, out_shape=(jax.ShapeDtypeStruct((n_dates, own, n_r...  1.68 us

profile of v2, /device:TPU:0, one launch (start us, length us, event | category | flops | bytes accessed | tf_op | source)
XLA Modules:
  0.0 34.0 jit_solution(4347523316919052544)
XLA Ops:
  0.6 0.0 copy-start.1
  0.6 0.0 copy-start.3
  0.7 0.0 copy-start.4
  0.7 0.0 copy-start.7
  0.7 0.9 %copy.14 = bf16[2,32,4,128]{3,1,0,2:T(8,128)(2,1)S(1)} copy(bf16[2,32,4,128]{3,2,1,0:T(4,128)(2,1)} %param.13) | data formatting | bytes 131072 | tf_op args[6]
  1.6 0.0 copy-start.8
  1.6 0.0 copy-start.9
  1.6 0.0 copy-done.1
  1.6 0.0 copy-done.3
  1.6 0.0 copy-done.4
  1.6 0.0 copy-done.7
  1.6 0.6 %copy-done.8 = s32[8,1]{0,1:T(1,128)S(1)} copy-done((s32[8,1]{0,1:T(1,128)S(1)}, s32[8,1]{0,1:T(1,128)}, u32[]{:S(2)}) %copy-start.8) | copy-done | bytes 56
  2.2 0.0 copy-done.9
  2.2 27.6 %shard_map.110 = (bf16[2,4,32,128]{3,2,1,0:T(8,128)(2,1)S(1)}, f32[12,128]{1,0:T(8,128)S(1)}, bf16[24,16,128]{2,1,0:T(8,128)(2,1)S(1)}, f32[2,12,128]{2,1,0:T(8,128)S(1)}) custom-call(s32[1,8]{1,0:T(1,128)S(1)} %bitcast.18, s32[8]{0:T(128)S(1)} %copy-done.9, bf16[12,8,128]{2,1,0:T(8,128)(2,1)S(1)} %bitcast.16, bf16[12,128]{1,0:T(8,128)(2,1)S(1)} %copy-done.7, ...), custom_call_target="tpu_custom_call" | custom-call | tf_op jit(solution)/shard_map/pallas_call | solution.py:467
  29.8 0.0 copy-start
  29.8 0.6 %copy-done = bf16[24,16,128]{2,1,0:T(8,128)(2,1)} copy-done((bf16[24,16,128]{2,1,0:T(8,128)(2,1)}, bf16[24,16,128]{2,1,0:T(8,128)(2,1)S(1)}, u32[]{:S(2)}) %copy-start) | copy-done | bytes 98328
  30.5 0.0 copy-start.2
  30.5 0.6 %copy-done.2 = bf16[2,4,32,128]{3,2,1,0:T(8,128)(2,1)} copy-done((bf16[2,4,32,128]{3,2,1,0:T(8,128)(2,1)}, bf16[2,4,32,128]{3,2,1,0:T(8,128)(2,1)S(1)}, u32[]{:S(2)}) %copy-start.2) | copy-done | bytes 65560
  31.1 0.0 copy-start.5
  31.1 0.6 %copy-done.5 = f32[2,12,128]{2,1,0:T(8,128)} copy-done((f32[2,12,128]{2,1,0:T(8,128)}, f32[2,12,128]{2,1,0:T(8,128)S(1)}, u32[]{:S(2)}) %copy-start.5) | copy-done | bytes 12312
  31.7 0.0 copy-start.6
  31.7 0.6 %copy-done.6 = f32[12,128]{1,0:T(8,128)} copy-done((f32[12,128]{1,0:T(8,128)}, f32[12,128]{1,0:T(8,128)S(1)}, u32[]{:S(2)}) %copy-start.6) | copy-done | bytes 6168
  32.3 1.7 %shard_map.111 = (bf16[2,32,4,128]{3,2,1,0:T(4,128)(2,1)}, f32[12,128]{1,0:T(8,128)}, f32[9,32,128]{2,1,0:T(8,128)}, f32[3,32,128]{2,1,0:T(8,128)}, f32[12,2,128]{2,1,0:T(2,128)}) custom-call(bf16[2,4,32,128]{3,2,1,0:T(8,128)(2,1)} %copy-done.2, f32[12,128]{1,0:T(8,128)} %copy-done.6, bf16[24,16,128]{2,1,0:T(8,128)(2,1)} %copy-done, f32[2,12,128]{2,1,0:T(8,128)} %copy-done.5), custom_call_target="tpu_custom_call" | custom-call | tf_op jit(solution)/shard_map/pallas_call | solution.py:506
Async XLA Ops:
  0.6 1.0 %copy-start.1 = (bf16[3,3,128,32]{2,3,1,0:T(8,128)(2,1)S(1)}, bf16[3,3,128,32]{2,3,1,0:T(8,128)(2,1)}, u32[]{:S(2)}) copy-start(bf16[3,3,128,32]{2,3,1,0:T(8,128)(2,1)} %param.11) | copy-start | bytes 221188
  0.6 1.0 %copy-start.3 = (bf16[8,12,128]{2,0,1:T(8,128)(2,1)S(1)}, bf16[8,12,128]{2,0,1:T(8,128)(2,1)}, u32[]{:S(2)}) copy-start(bf16[8,12,128]{2,0,1:T(8,128)(2,1)} %param.7) | copy-start | bytes 73732
  0.7 1.0 %copy-start.4 = (bf16[3,128,32]{1,2,0:T(8,128)(2,1)S(1)}, bf16[3,128,32]{1,2,0:T(8,128)(2,1)}, u32[]{:S(2)}) copy-start(bf16[3,128,32]{1,2,0:T(8,128)(2,1)} %param.12) | copy-start | bytes 73732
  0.7 1.0 %copy-start.7 = (bf16[12,128]{1,0:T(8,128)(2,1)S(1)}, bf16[12,128]{1,0:T(8,128)(2,1)}, u32[]{:S(2)}) copy-start(bf16[12,128]{1,0:T(8,128)(2,1)} %stem_ref.1) | copy-start | bytes 9220
  1.6 0.7 %copy-start.8 = (s32[8,1]{0,1:T(1,128)S(1)}, s32[8,1]{0,1:T(1,128)}, u32[]{:S(2)}) copy-start(s32[8,1]{0,1:T(1,128)} %param.8) | copy-start | bytes 100
  1.6 0.7 %copy-start.9 = (s32[8]{0:T(128)S(1)}, s32[8]{0:T(128)}, u32[]{:S(2)}) copy-start(s32[8]{0:T(128)} %date_ref.1) | copy-start | bytes 100
  29.8 0.6 %copy-start = (bf16[24,16,128]{2,1,0:T(8,128)(2,1)}, bf16[24,16,128]{2,1,0:T(8,128)(2,1)S(1)}, u32[]{:S(2)}) copy-start(bf16[24,16,128]{2,1,0:T(8,128)(2,1)S(1)} %get-tuple-element.16.grad_in) | copy-start | bytes 294916
  30.5 0.6 %copy-start.2 = (bf16[2,4,32,128]{3,2,1,0:T(8,128)(2,1)}, bf16[2,4,32,128]{3,2,1,0:T(8,128)(2,1)S(1)}, u32[]{:S(2)}) copy-start(bf16[2,4,32,128]{3,2,1,0:T(8,128)(2,1)S(1)} %get-tuple-element.14.fo_in) | copy-start | bytes 196612
  31.1 0.6 %copy-start.5 = (f32[2,12,128]{2,1,0:T(8,128)}, f32[2,12,128]{2,1,0:T(8,128)S(1)}, u32[]{:S(2)}) copy-start(f32[2,12,128]{2,1,0:T(8,128)S(1)} %get-tuple-element.17.bg_in) | copy-start | bytes 36868
  31.7 0.6 %copy-start.6 = (f32[12,128]{1,0:T(8,128)}, f32[12,128]{1,0:T(8,128)S(1)}, u32[]{:S(2)}) copy-start(f32[12,128]{1,0:T(8,128)S(1)} %get-tuple-element.15.gstem_in) | copy-start | bytes 18436

commit v3 on v2

--- a/solution.py
+++ b/solution.py
@@ -49,7 +49,7 @@
 def kernel(
     n, nf, bp, scale,
     tile_ref, date_ref, panels_ref, stem_ref, ws_ref, wtm_ref, cot_ref,
-    fo_ref, gstem_ref, grad_ref, bg_ref,
+    res_ref,
     pp, pan_out, pan_in, raw, wall, wback, stem16, stem_t, cot, feat, act, pre_g, pg3,
     rs_out, rs_in, ag, sa_out, sa, sb_out, sb,
     pan_s, pan_r, raw_s, raw_r, w_s, w_r, c_s, c_r, lo_s, lo_r, hi_s, hi_r,
@@ -95,6 +95,9 @@
     mine = pl.ds(pl.multiple_of(f * own, own), own)
     for q in range(12):
         wall[mine, q * chan : (q + 1) * chan] = ws_ref[q] if q < 9 else wtm_ref[q - 9]
+    for t in range(2):
+        for r in range(4):
+            cot[1 + r, t, mine, :] = cot_ref[r, t]
     pad_rows = lax.broadcasted_iota(jnp.int32, (n_slots, 16, cols), 1)
     pp[...] = jnp.where(pad_rows == bands, 1.0, 0.0)
     for b in range(bands):
@@ -146,7 +149,7 @@
         return remote(wall.at[mine], wall.at[mine], w_s.at[slot], w_r.at[f], (j, to))
 
     def c_copy(to, slot):
-        return remote(cot_ref, cot.at[pl.ds(1, 4), :, mine, :], c_s.at[slot], c_r.at[f], (j, to))
+        return remote(cot.at[pl.ds(1, 4), :, mine, :], cot.at[pl.ds(1, 4), :, mine, :], c_s.at[slot], c_r.at[f], (j, to))
 
     def w_forward():
         at = wall.at[group(par)]
@@ -161,13 +164,13 @@
 
     def c_wait(g):
         at = cot.at[pl.ds(1, 4), :, group(g), :]
-        remote(cot_ref, at, c_s.at[0], c_r.at[g], (j, par)).wait_recv()
+        remote(cot.at[pl.ds(1, 4), :, mine, :], at, c_s.at[0], c_r.at[g], (j, par)).wait_recv()
 
     def lo_copy(d):
-        return remote(cot_ref.at[3], cot.at[0, :, mine, :], lo_s.at[d], lo_r.at[f], (j + 1, fpeer(d)))
+        return remote(cot.at[4, :, mine, :], cot.at[0, :, mine, :], lo_s.at[d], lo_r.at[f], (j + 1, fpeer(d)))
 
     def hi_copy(d):
-        return remote(cot_ref.at[0], cot.at[5, :, mine, :], hi_s.at[d], hi_r.at[f], (j - 1, fpeer(d)))
+        return remote(cot.at[1, :, mine, :], cot.at[5, :, mine, :], hi_s.at[d], hi_r.at[f], (j - 1, fpeer(d)))
 
     w_copy(par, 0).start()
     w_copy(sib, 1).start()
@@ -184,7 +187,6 @@
         for d in range(nf):
             hi_copy(d).start()
 
-    cot[1:5, :, mine, :] = cot_ref[...]
     stem_t[...] = jnp.zeros((cols, chan), F32)
     stem_t[0:bands, :] = stem_ref[...].astype(F32)
     stem16[...] = stem_t[0:16, :].astype(BF16)
@@ -268,12 +270,12 @@
     @pl.when(j > 0)
     def _():
         for g in range(nf):
-            remote(cot_ref.at[3], cot.at[0, :, g * own : (g + 1) * own, :], lo_s.at[g], lo_r.at[g], (j - 1, g)).wait_recv()
+            remote(cot.at[4, :, mine, :], cot.at[0, :, g * own : (g + 1) * own, :], lo_s.at[g], lo_r.at[g], (j - 1, g)).wait_recv()
 
     @pl.when(j < n - 1)
     def _():
         for g in range(nf):
-            remote(cot_ref.at[0], cot.at[5, :, g * own : (g + 1) * own, :], hi_s.at[g], hi_r.at[g], (j + 1, g)).wait_recv()
+            remote(cot.at[1, :, mine, :], cot.at[5, :, g * own : (g + 1) * own, :], hi_s.at[g], hi_r.at[g], (j + 1, g)).wait_recv()
 
     cot_rows = jnp.concatenate([cot[r].reshape(2 * chan, cols) for r in range(6)], axis=1)
     lane = lax.broadcasted_iota(jnp.int32, (chan, 6 * cols), 1)
@@ -295,7 +297,7 @@
             rs_out[b // bp, (b % bp) * 16 : (b % bp) * 16 + 16, :] = grad[h * 16 : h * 16 + 16].astype(BF16)
 
     cot_own = [
-        jnp.concatenate([cot_ref[r, t] for r in range(4)], axis=1) for t in range(2)
+        jnp.concatenate([cot[1 + r, t, mine, :] for r in range(4)], axis=1) for t in range(2)
     ]
     act0, act1 = act[0:chan, :], act[chan : 2 * chan, :]
     put(9, dot_t(cot_own[1], act0) * scale)
@@ -347,7 +349,7 @@
     sa[f] = sa_out[...]
     bgrad = dot(stem16[...], upper) + dot(stem16[...], lower)
     for t in range(2):
-        bg_ref[t] = bgrad[0:bands, t * cols : (t + 1) * cols]
+        res_ref[656 + t * 16 : 672 + t * 16, :] = bgrad[:, t * cols : (t + 1) * cols]
 
     wt_time = wall[mine, 9 * chan : 12 * chan]
     feat_own = pl.ds(pl.multiple_of(chan + f * own, own), own)
@@ -355,7 +357,8 @@
         out = dot(wt_time[:, (1 - t) * chan : (3 - t) * chan], act[...])
         out = out + feat[feat_own, t * 1024 + 256 : t * 1024 + 768].astype(F32)
         for r in range(4):
-            fo_ref[t, r] = out[:, r * cols : (r + 1) * cols].astype(BF16)
+            at = (t * 4 + r) * own
+            res_ref[at : at + own, :] = out[:, r * cols : (r + 1) * cols]
 
     for d in range(1, nf):
         g = fpeer(d)
@@ -420,7 +423,7 @@
         remote(sb_out, sb.at[k], sb_s.at[d], sb_r.at[k], (k, f)).wait_recv()
 
     loop(n - 1, lambda d: sb_wait(d + 1))
-    gstem_ref[...] = total(n, lambda k: sb[k])[0:bands]
+    res_ref[640:656, :] = total(n, lambda k: sb[k])
 
     def ag_wait(d):
         k = tpeer(d)
@@ -428,24 +431,25 @@
 
     loop(n - 1, lambda d: ag_wait(d + 1))
     for b in range(24):
-        grad_ref[b] = ag[b // bp, (b % bp) * 16 : (b % bp) * 16 + 16, :]
+        block = ag[b // bp, (b % bp) * 16 : (b % bp) * 16 + 16, :]
+        res_ref[256 + b * 16 : 272 + b * 16, :] = block.astype(F32)
     loop(n - 1, lambda d: ag_copy(d + 1).wait_send())
     loop(n - 1, lambda d: sb_copy(d + 1).wait_send())
 
 
-def finish(fo_in, gstem_in, grad_in, bg_in, fo_ref, gstem_ref, gsp_ref, gtm_ref, bg_ref):
-    for t in range(2):
-        fo_ref[t] = jnp.swapaxes(fo_in[t].astype(F32), 0, 1).astype(BF16)
-    gstem_ref[...] = gstem_in[...]
-    for t in range(2):
-        bg_ref[:, t, :] = bg_in[t]
+def finish(res_ref, fo_ref, gstem_ref, gsp_ref, gtm_ref, bg_ref):
+    bands = gstem_ref.shape[0]
+    for t in range(2):
+        part = res_ref[t * 128 : t * 128 + 128, :].reshape(4, 32, res_ref.shape[1])
+        fo_ref[t] = jnp.swapaxes(part, 0, 1).astype(BF16)
+        bg_ref[:, t, :] = res_ref[656 + t * 16 : 656 + t * 16 + bands, :]
+    gstem_ref[...] = res_ref[640 : 640 + bands, :]
     for q in range(12):
-        for h in range(2):
-            block = grad_in[2 * q + h].astype(F32)
-            if q < 9:
-                gsp_ref[q, h * 16 : h * 16 + 16, :] = block
-            else:
-                gtm_ref[q - 9, h * 16 : h * 16 + 16, :] = block
+        block = res_ref[256 + q * 32 : 288 + q * 32, :]
+        if q < 9:
+            gsp_ref[q] = block
+        else:
+            gtm_ref[q - 9] = block
 
 
 def per_device(
@@ -460,20 +464,14 @@
     scale = 1.0 / math.sqrt(n_dates * n_rows * n * cols)
     ws = spatial_weight.transpose(0, 1, 3, 2).reshape(9, own, chan)
     wtm = temporal_weight.transpose(0, 2, 1)
-    cot = cotangent.transpose(2, 0, 1, 3)
     dma = pltpu.SemaphoreType.DMA
     vmem = pl.BlockSpec(memory_space=pltpu.VMEM)
     smem = pl.BlockSpec(memory_space=pltpu.SMEM)
     out = pl.pallas_call(
         functools.partial(kernel, n, nf, bp, scale),
-        out_shape=(
-            jax.ShapeDtypeStruct((n_dates, n_rows, own, cols), BF16),
-            jax.ShapeDtypeStruct((n_bands, chan), F32),
-            jax.ShapeDtypeStruct((24, 16, cols), BF16),
-            jax.ShapeDtypeStruct((n_dates, n_bands, cols), F32),
-        ),
+        out_shape=jax.ShapeDtypeStruct((688, cols), F32),
         in_specs=[smem, smem, vmem, vmem, vmem, vmem, vmem],
-        out_specs=(vmem,) * 4,
+        out_specs=vmem,
         scratch_shapes=[
             pltpu.VMEM((n_slots, 16, cols), F32),
             pltpu.VMEM((n, 32, cols), BF16),
@@ -502,7 +500,7 @@
         compiler_params=pltpu.CompilerParams(
             collective_id=0, has_side_effects=True, vmem_limit_bytes=40 * 1024 * 1024
         ),
-    )(panel_tile.T, panel_date, panels.transpose(1, 0, 2), stem_weight, ws, wtm, cot)
+    )(panel_tile.T, panel_date, panels.transpose(1, 0, 2), stem_weight, ws, wtm, cotangent.transpose(2, 0, 1, 3))
     features_out, grad_stem, gsp, gtm, bg = pl.pallas_call(
         finish,
         out_shape=(
@@ -512,9 +510,9 @@
             jax.ShapeDtypeStruct((3, own, chan), F32),
             jax.ShapeDtypeStruct((n_bands, n_dates, cols), F32),
         ),
-        in_specs=[vmem] * 4,
+        in_specs=[vmem],
         out_specs=(vmem,) * 5,
-    )(*out)
+    )(out)
     return (
         features_out,
         grad_stem,

time: 34.2 us -> 32.5 us (0.950)
  local copies, waits for them, and re-layouts: 3.98 us -> 2.25 us
    unnamed x21 -> x15, local copies, waits for them, and re-layouts: 3.98 us -> 2.25 us
where the time goes in v3:
time: 32.5 us; the launch traced here: 32.3 us
  Pallas kernels  29.3 us (90%)
  local copies, waits for them, and re-layouts  2.25 us (7%)
  between operations  0.73 us (2%)
    pallas_call x1, Pallas kernels, per_device(): pl.pallas_call(functools.partial(kernel, n, nf, bp, scale), out_shape=jax...  27.6 us
    unnamed x15, local copies, waits for them, and re-layouts  2.25 us
    pallas_call x1, Pallas kernels, per_device(): pl.pallas_call(finish, out_shape=(jax.ShapeDtypeStruct((n_dates, own, n_r...  1.69 us

profile of v3, /device:TPU:0, one launch (start us, length us, event | category | flops | bytes accessed | tf_op | source)
XLA Modules:
  0.0 32.3 jit_solution(10501323559470847790)
XLA Ops:
  0.6 0.0 copy-start.1
  0.6 0.0 copy-start.2
  0.7 0.0 copy-start.3
  0.7 0.0 copy-start.4
  0.7 0.9 %copy.14 = bf16[2,32,4,128]{3,1,0,2:T(8,128)(2,1)S(1)} copy(bf16[2,32,4,128]{3,2,1,0:T(4,128)(2,1)} %param.13) | data formatting | bytes 131072 | tf_op args[6]
  1.6 0.0 copy-start.5
  1.6 0.0 copy-start.6
  1.6 0.0 copy-done.1
  1.6 0.0 copy-done.2
  1.6 0.0 copy-done.3
  1.6 0.0 copy-done.4
  1.6 0.6 %copy-done.5 = s32[8,1]{0,1:T(1,128)S(1)} copy-done((s32[8,1]{0,1:T(1,128)S(1)}, s32[8,1]{0,1:T(1,128)}, u32[]{:S(2)}) %copy-start.5) | copy-done | bytes 56
  2.2 0.0 copy-done.6
  2.2 27.6 %shard_map.110.res_ref = f32[688,128]{1,0:T(8,128)S(1)} custom-call(s32[1,8]{1,0:T(1,128)S(1)} %bitcast.18, s32[8]{0:T(128)S(1)} %copy-done.6, bf16[12,8,128]{2,1,0:T(8,128)(2,1)S(1)} %bitcast.16, bf16[12,128]{1,0:T(8,128)(2,1)S(1)} %copy-done.4, bf16[9,32,128]{2,1,0:T(8,128)(2,1)S(1)} %bitcast.15, bf16[3,32,128]{2,1,0:T(8,128)(2,1)S(1)} %bitcast.17, ...), custom_call_target="tpu_custom_call" | custom-call | tf_op jit(solution)/shard_map/pallas_call | solution.py:470
  29.8 0.0 copy-start
  29.9 0.7 %copy-done = f32[688,128]{1,0:T(8,128)} copy-done((f32[688,128]{1,0:T(8,128)}, f32[688,128]{1,0:T(8,128)S(1)}, u32[]{:S(2)}) %copy-start) | copy-done | bytes 352280
  30.6 1.7 %shard_map.111 = (bf16[2,32,4,128]{3,2,1,0:T(4,128)(2,1)}, f32[12,128]{1,0:T(8,128)}, f32[9,32,128]{2,1,0:T(8,128)}, f32[3,32,128]{2,1,0:T(8,128)}, f32[12,2,128]{2,1,0:T(2,128)}) custom-call(f32[688,128]{1,0:T(8,128)} %copy-done), custom_call_target="tpu_custom_call" | custom-call | tf_op jit(solution)/shard_map/pallas_call | solution.py:504
Async XLA Ops:
  0.6 1.0 %copy-start.1 = (bf16[3,3,128,32]{2,3,1,0:T(8,128)(2,1)S(1)}, bf16[3,3,128,32]{2,3,1,0:T(8,128)(2,1)}, u32[]{:S(2)}) copy-start(bf16[3,3,128,32]{2,3,1,0:T(8,128)(2,1)} %param.11) | copy-start | bytes 221188
  0.6 1.0 %copy-start.2 = (bf16[8,12,128]{2,0,1:T(8,128)(2,1)S(1)}, bf16[8,12,128]{2,0,1:T(8,128)(2,1)}, u32[]{:S(2)}) copy-start(bf16[8,12,128]{2,0,1:T(8,128)(2,1)} %param.7) | copy-start | bytes 73732
  0.7 1.0 %copy-start.3 = (bf16[3,128,32]{1,2,0:T(8,128)(2,1)S(1)}, bf16[3,128,32]{1,2,0:T(8,128)(2,1)}, u32[]{:S(2)}) copy-start(bf16[3,128,32]{1,2,0:T(8,128)(2,1)} %param.12) | copy-start | bytes 73732
  0.7 1.0 %copy-start.4 = (bf16[12,128]{1,0:T(8,128)(2,1)S(1)}, bf16[12,128]{1,0:T(8,128)(2,1)}, u32[]{:S(2)}) copy-start(bf16[12,128]{1,0:T(8,128)(2,1)} %stem_ref.1) | copy-start | bytes 9220
  1.6 0.7 %copy-start.5 = (s32[8,1]{0,1:T(1,128)S(1)}, s32[8,1]{0,1:T(1,128)}, u32[]{:S(2)}) copy-start(s32[8,1]{0,1:T(1,128)} %param.8) | copy-start | bytes 100
  1.6 0.7 %copy-start.6 = (s32[8]{0:T(128)S(1)}, s32[8]{0:T(128)}, u32[]{:S(2)}) copy-start(s32[8]{0:T(128)} %date_ref.1) | copy-start | bytes 100
  29.8 0.7 %copy-start = (f32[688,128]{1,0:T(8,128)}, f32[688,128]{1,0:T(8,128)S(1)}, u32[]{:S(2)}) copy-start(f32[688,128]{1,0:T(8,128)S(1)} %shard_map.110.res_ref) | copy-start | bytes 1056772

commit v4 on v3

--- a/solution.py
+++ b/solution.py
@@ -498,7 +498,7 @@
             dma((n,)), dma((n,)), dma((n,)), dma((n,)), dma((nf,)), dma((nf,)), dma((n,)), dma((n,)),
         ],
         compiler_params=pltpu.CompilerParams(
-            collective_id=0, has_side_effects=True, vmem_limit_bytes=40 * 1024 * 1024
+            collective_id=0, has_side_effects=True, vmem_limit_bytes=16 * 1024 * 1024
         ),
     )(panel_tile.T, panel_date, panels.transpose(1, 0, 2), stem_weight, ws, wtm, cotangent.transpose(2, 0, 1, 3))
     features_out, grad_stem, gsp, gtm, bg = pl.pallas_call(
@@ -512,6 +512,7 @@
         ),
         in_specs=[vmem],
         out_specs=(vmem,) * 5,
+        compiler_params=pltpu.CompilerParams(vmem_limit_bytes=8 * 1024 * 1024),
     )(out)
     return (
         features_out,

time: 32.5 us -> 30.7 us (0.945)
  Pallas kernels: 29.3 us -> 28.3 us
  local copies, waits for them, and re-layouts: 2.25 us -> 1.53 us
    pallas_call x1, Pallas kernels: 1.69 us -> 0.73 us  [per_device(): pl.pallas_call(finish, out_shape=(jax.ShapeDtypeStruct((n_dates, own, n_r...]
    unnamed x15 -> x13, local copies, waits for them, and re-layouts: 2.25 us -> 1.53 us
where the time goes in v4:
time: 30.7 us; the launch traced here: 30.6 us
  Pallas kernels  28.3 us (92%)
  local copies, waits for them, and re-layouts  1.53 us (5%)
  between operations  0.72 us (2%)
    pallas_call x1, Pallas kernels, per_device(): pl.pallas_call(functools.partial(kernel, n, nf, bp, scale), out_shape=jax...  27.6 us
    unnamed x13, local copies, waits for them, and re-layouts  1.53 us
    pallas_call x1, Pallas kernels, per_device(): pl.pallas_call(finish, out_shape=(jax.ShapeDtypeStruct((n_dates, own, n_r...  0.73 us

profile of v4, /device:TPU:0, one launch (start us, length us, event | category | flops | bytes accessed | tf_op | source)
XLA Modules:
  0.0 30.6 jit_solution(10933114532259827853)
XLA Ops:
  0.6 0.0 copy-start
  0.6 0.0 copy-start.1
  0.7 0.0 copy-start.2
  0.7 0.0 copy-start.3
  0.7 0.9 %copy.14 = bf16[2,32,4,128]{3,1,0,2:T(8,128)(2,1)S(1)} copy(bf16[2,32,4,128]{3,2,1,0:T(4,128)(2,1)} %param.13) | data formatting | bytes 131072 | tf_op args[6]
  1.6 0.0 copy-start.4
  1.6 0.0 copy-start.5
  1.6 0.0 copy-done
  1.6 0.0 copy-done.1
  1.6 0.0 copy-done.2
  1.6 0.0 copy-done.3
  1.6 0.6 %copy-done.4 = s32[8,1]{0,1:T(1,128)S(1)} copy-done((s32[8,1]{0,1:T(1,128)S(1)}, s32[8,1]{0,1:T(1,128)}, u32[]{:S(2)}) %copy-start.4) | copy-done | bytes 56
  2.2 0.0 copy-done.5
  2.2 27.6 %shard_map.110.res_ref = f32[688,128]{1,0:T(8,128)S(1)} custom-call(s32[1,8]{1,0:T(1,128)S(1)} %bitcast.18, s32[8]{0:T(128)S(1)} %copy-done.5, bf16[12,8,128]{2,1,0:T(8,128)(2,1)S(1)} %bitcast.16, bf16[12,128]{1,0:T(8,128)(2,1)S(1)} %copy-done.3, bf16[9,32,128]{2,1,0:T(8,128)(2,1)S(1)} %bitcast.15, bf16[3,32,128]{2,1,0:T(8,128)(2,1)S(1)} %bitcast.17, ...), custom_call_target="tpu_custom_call" | custom-call | tf_op jit(solution)/shard_map/pallas_call | solution.py:470
  29.8 0.7 %shard_map.111 = (bf16[2,32,4,128]{3,2,1,0:T(4,128)(2,1)}, f32[12,128]{1,0:T(8,128)}, f32[9,32,128]{2,1,0:T(8,128)}, f32[3,32,128]{2,1,0:T(8,128)}, f32[12,2,128]{2,1,0:T(2,128)}) custom-call(f32[688,128]{1,0:T(8,128)S(1)} %shard_map.110.res_ref), custom_call_target="tpu_custom_call" | custom-call | tf_op jit(solution)/shard_map/pallas_call | solution.py:504
Async XLA Ops:
  0.6 1.0 %copy-start = (bf16[3,3,128,32]{2,3,1,0:T(8,128)(2,1)S(1)}, bf16[3,3,128,32]{2,3,1,0:T(8,128)(2,1)}, u32[]{:S(2)}) copy-start(bf16[3,3,128,32]{2,3,1,0:T(8,128)(2,1)} %param.11) | copy-start | bytes 221188
  0.6 1.0 %copy-start.1 = (bf16[8,12,128]{2,0,1:T(8,128)(2,1)S(1)}, bf16[8,12,128]{2,0,1:T(8,128)(2,1)}, u32[]{:S(2)}) copy-start(bf16[8,12,128]{2,0,1:T(8,128)(2,1)} %param.7) | copy-start | bytes 73732
  0.7 1.0 %copy-start.2 = (bf16[3,128,32]{1,2,0:T(8,128)(2,1)S(1)}, bf16[3,128,32]{1,2,0:T(8,128)(2,1)}, u32[]{:S(2)}) copy-start(bf16[3,128,32]{1,2,0:T(8,128)(2,1)} %param.12) | copy-start | bytes 73732
  0.7 1.0 %copy-start.3 = (bf16[12,128]{1,0:T(8,128)(2,1)S(1)}, bf16[12,128]{1,0:T(8,128)(2,1)}, u32[]{:S(2)}) copy-start(bf16[12,128]{1,0:T(8,128)(2,1)} %stem_ref.1) | copy-start | bytes 9220
  1.6 0.7 %copy-start.4 = (s32[8,1]{0,1:T(1,128)S(1)}, s32[8,1]{0,1:T(1,128)}, u32[]{:S(2)}) copy-start(s32[8,1]{0,1:T(1,128)} %param.8) | copy-start | bytes 100
  1.6 0.7 %copy-start.5 = (s32[8]{0:T(128)S(1)}, s32[8]{0:T(128)}, u32[]{:S(2)}) copy-start(s32[8]{0:T(128)} %date_ref.1) | copy-start | bytes 100
